TPU v7x, 32 devices: a whole 2x2x4 slice. The times are simulated.
32 devices in a mesh: img: 2 (over y), az: 8 (over z, x), rg: 2 (over core).
Axes of the slice: x: 2, y: 2, z: 4, core: 2. Of those that a mesh axis runs over, the one named last changes fastest.
Arguments:
- history: float32 [2, 2048, 2048], P(None, ('img', 'rg'), 'az'), parts along dimension 1, may hold values from -6 to 6
- coeffs: float32 [1024, 384], P('rg'), may hold values from -0.625 to 0.625
- band_width: int32 [1024], P('rg'), may hold values from 1 to 48, as said below
- block_shift: int32 [8], P('rg'), may hold values from -32 to 32, as said below
- scatter_rows: int32 [128], P('img'), parts along dimension 0, may hold values from 0 to 1023
- window_width: int32 [128], P('img'), parts along dimension 0, may hold values from 8 to 128, as said below
Outputs:
- spectrum: float32 [2, 2048, 2048], P(None, ('img', 'rg'), 'az'), parts along dimension 1
- phase: float32 [4096], P(('img', 'az')), parts along dimension 0
There are 2 independent parts, one for each index of `img`. A program takes and returns all parts, laid end to end along the dimension named above; an argument that names none is the same for every part. Nothing has to cross between parts.
Inputs may be any that keep to these rules, and one draw needn't show every extreme that they name: `band_width`: the largest half-width 48 is taken by some row and the smallest, 1, by another. `block_shift`: offsets 32 and -32 both occur. `window_width`: Half-widths 128 and 8 both occur.
All inputs are finite; a program needn't handle non-finite values.
Results may differ from a plain program's by a relative error of at most 0.0003.
Values sent between devices are 32-bit elements; how exact they have to be, the bound alone decides.
A program may use at most 64 MiB of HBM per device.

v0:
```python
import math

import jax
import jax.numpy as jnp
from jax import lax
from jax.sharding import PartitionSpec as P

BLOCK = 128
S = 64


def extended(cells, sides, width):
    for axis, dim in sides:
        count = lax.axis_size(axis)
        ends = count - 1
        head = lax.slice_in_dim(cells, 0, width, axis=dim)
        tail = lax.slice_in_dim(cells, cells.shape[dim] - width, cells.shape[dim], axis=dim)
        cells = jnp.concatenate(
            [
                lax.ppermute(tail, axis, [(i, (i + 1) % count) for i in range(ends)]),
                cells,
                lax.ppermute(head, axis, [((i + 1) % count, i) for i in range(ends)]),
            ],
            axis=dim,
        )
    return cells


def swapped(block, axis, bit):
    count = lax.axis_size(axis)
    route = []
    for low in range(count):
        high = low | 1 << bit
        if high != low and high < count:
            route += [(low, high), (high, low)]
    return lax.ppermute(block, axis, route)


def broadcast(value, axis, source):
    kept = jnp.where(lax.axis_index(axis) == source, value, 0).astype(value.dtype)
    return lax.psum(kept, axis)


def shifted(block, axis, distance):
    devices = range(lax.axis_size(axis))
    route = [((i - distance) % len(devices), i) for i in devices]
    return lax.ppermute(block, axis, route)


def entering(part, axis, combine, identity):
    place = lax.axis_index(axis)
    gathered = lax.all_gather(part, axis)
    state = jnp.zeros_like(part) + jnp.asarray(identity, part.dtype)

    def one(hop, state):
        return combine(state, lax.dynamic_index_in_dim(gathered, hop, 0, False))

    return lax.fori_loop(0, place, one, state)


def bit_flip(values, bits):
    flipped = jnp.zeros_like(values)
    for bit in range(bits):
        flipped = flipped | (values >> bit & 1) << bits - 1 - bit
    return flipped


def tables(first_index, second_index, length):
    angle = (first_index[:, None] * second_index[None, :] % length).astype(jnp.float32) * (
        2.0 * math.pi / length
    )
    return (jnp.cos(angle), jnp.sin(angle))


def shards(history, coeffs, band_width, block_shift, scatter_rows, window_width):
    rows_dev = history.shape[1]
    cols = history.shape[2]
    panels = lax.axis_size("az")
    sections = panels.bit_length() - 1
    total_cols = cols * panels
    range_me = lax.axis_index("rg")
    az_me = lax.axis_index("az")
    nblocks = rows_dev // BLOCK
    high = lax.Precision.HIGHEST
    padded = extended(history, (("rg", 1),), BLOCK)
    local_rows = jnp.arange(rows_dev, dtype=jnp.int32)
    global_rows = range_me * rows_dev + local_rows
    local_blocks = local_rows // BLOCK
    global_blocks = range_me * nblocks + local_blocks
    offsets = jnp.arange(3 * BLOCK, dtype=jnp.int32)
    source = BLOCK * (global_blocks - 1)[:, None] + offsets[None, :]
    keep = (
        jnp.abs(source - global_rows[:, None] - block_shift[local_blocks][:, None])
        <= band_width[:, None]
    )
    weights = jnp.where(keep, coeffs, jnp.zeros_like(coeffs)).reshape(nblocks, BLOCK, 3 * BLOCK)
    stacked = padded.reshape(2, nblocks + 2, BLOCK, cols)
    windows = jnp.concatenate([stacked[:, :-2], stacked[:, 1:-1], stacked[:, 2:]], axis=2)
    resampled = jnp.einsum("bit,cbtn->cbin", weights, windows, precision=high).reshape(
        2 * rows_dev, cols
    )
    local_index = jnp.arange(cols, dtype=jnp.int32)
    cosine, sine = tables(local_index, local_index, cols)
    product = jnp.dot(resampled, jnp.concatenate([cosine, sine], axis=1), precision=high)
    real_cos = product[:rows_dev, :cols]
    real_sin = product[:rows_dev, cols:]
    imag_cos = product[rows_dev:, :cols]
    imag_sin = product[rows_dev:, cols:]
    part_real = real_cos + imag_sin
    part_imag = imag_cos - real_sin
    sample_base = bit_flip(az_me, sections)
    twist = (sample_base * local_index % total_cols).astype(jnp.float32) * (
        -2.0 * math.pi / total_cols
    )
    twist_cos = jnp.cos(twist)
    twist_sin = jnp.sin(twist)
    state_real = part_real * twist_cos - part_imag * twist_sin
    state_imag = part_real * twist_sin + part_imag * twist_cos
    state = jnp.stack([state_real, state_imag])
    for section in range(sections):
        half = 1 << section
        partner = swapped(state, "az", section)
        lowbit = az_me >> section & 1 == 0
        lower = jnp.where(lowbit, state, partner)
        upper = jnp.where(lowbit, partner, state)
        angle = (az_me % half).astype(jnp.float32) * (-math.pi / half)
        turn_cos = jnp.cos(angle)
        turn_sin = jnp.sin(angle)
        moved_real = upper[0] * turn_cos - upper[1] * turn_sin
        moved_imag = upper[0] * turn_sin + upper[1] * turn_cos
        moved = jnp.stack([moved_real, moved_imag])
        state = jnp.where(lowbit, lower + moved, lower - moved)
    selector = (scatter_rows[:, None] == global_rows[None, :]).astype(jnp.float32)
    picked = jnp.einsum("sr,crn->csn", selector, state, precision=high)
    freq = az_me * cols + local_index
    distance = jnp.minimum(freq, total_cols - freq)
    inside = distance[None, :] <= window_width[:, None]
    masked = jnp.where(inside[None], picked, jnp.zeros_like(picked))
    gathered_rows = lax.psum(masked, "rg")
    low_part = broadcast(gathered_rows, "az", 0)
    high_part = broadcast(gathered_rows, "az", panels - 1)
    sample = az_me * cols + local_index
    low_cos, low_sin = tables(local_index, sample, total_cols)
    high_cos, high_sin = tables(total_cols - cols + local_index, sample, total_cols)
    freq_table = jnp.concatenate(
        [
            jnp.concatenate([low_cos, low_sin], axis=1),
            jnp.concatenate([high_cos, high_sin], axis=1),
        ],
        axis=0,
    )
    windowed = jnp.concatenate([low_part, high_part], axis=2).reshape(2 * S, 2 * cols)
    signal = jnp.dot(windowed, freq_table, precision=high)
    signal_real = signal[:S, :cols] - signal[S:, cols:]
    signal_imag = signal[:S, cols:] + signal[S:, :cols]
    edge = jnp.stack([signal_real[:, 0], signal_imag[:, 0]])
    arriving = shifted(edge, "az", -1)
    next_real = jnp.concatenate([signal_real[:, 1:], arriving[0][:, None]], axis=1)
    next_imag = jnp.concatenate([signal_imag[:, 1:], arriving[1][:, None]], axis=1)
    numer = jnp.sum(signal_real * next_imag - signal_imag * next_real, axis=0)
    denom = jnp.sum(signal_real * signal_real + signal_imag * signal_imag, axis=0)
    grad = numer / (denom + 1e-06)
    running = jnp.cumsum(grad) - grad
    local_total = jnp.sum(grad, keepdims=True)
    before = entering(
        local_total, "az", lambda early, late: early + late, jnp.zeros((1,), jnp.float32)
    )[0]
    mean = lax.psum(local_total, "az")[0] / total_cols
    phase = before + running - sample.astype(jnp.float32) * mean
    return (state, phase)


def solution(mesh):
    in_specs = (P(None, ("img", "rg"), "az"), P("rg", None), P("rg"), P("rg"), P("img"), P("img"))
    out_specs = (P(None, ("img", "rg"), "az"), P(("img", "az")))
    return jax.shard_map(shards, mesh=mesh, in_specs=in_specs, out_specs=out_specs, check_vma=False)
```

profile of v0, /device:TPU:0, one launch (start us, length us, event | category | flops | bytes accessed | tf_op | source)
XLA Modules:
  0.0 264.9 jit_solution(10274810327666861524)
XLA Ops:
  7.2 1.1 fusion.63
  8.4 2.4 collective-permute-start
  10.7 1.3 collective-permute-start.1
  12.1 1.0 fusion.34
  13.1 1.4 fusion.64
  14.6 2.6 compare_select_fusion.1
  17.2 1.5 fusion.14
  19.2 2.2 fusion.2
  21.5 1.8 fusion.15
  23.6 2.4 collective-permute-start.2
  25.9 23.6 %collective-permute-done.2 = f32[2,512,256]{2,1,0:T(8,128)S(1)} collective-permute-done((f32[2,512,256]{2,1,0:T(8,128)S(1)}, f32[2,512,256]{2,1,0:T(8,128)S(1)}, u32[]{:S(2)}, u32[]{:S(2)}) %collective-permute-start.2) | collective-permute-done | bytes 1048608 | tf_op jit(solution)/shard_map/ppermute | solution.py:36
  49.8 1.3 subtract_select_fusion.2
  51.1 2.3 collective-permute-start.3
  53.6 23.6 %collective-permute-done.3 = f32[2,512,256]{2,1,0:T(8,128)} collective-permute-done((f32[2,512,256]{2,1,0:T(8,128)}, f32[2,512,256]{2,1,0:T(8,128)}, u32[]{:S(2)}, u32[]{:S(2)}) %collective-permute-start.3) | collective-permute-done | bytes 1048608 | tf_op jit(solution)/shard_map/ppermute | solution.py:36
  77.2 1.5 broadcast_select_fusion.1
  78.8 0.9 copy-done.1
  80.3 2.8 %collective-permute-start.4 = (f32[2,512,256]{2,1,0:T(8,128)S(1)}, f32[2,512,256]{2,1,0:T(8,128)S(1)}, u32[]{:S(2)}, u32[]{:S(2)}) collective-permute-start(f32[2,512,256]{2,1,0:T(8,128)S(1)} %subtract_select_fusion.1), channel_id=1, source_target_pairs={{0,8},{8,0},{2,10},{10,2},{4,12},{12,4},{6,14},{14,6},{1,9},{9,1},... | collective-permute-start | bytes 3145736 | tf_op jit(solution)/shard_map/ppermute | solution.py:36
  83.4 45.0 %collective-permute-done.4 = f32[2,512,256]{2,1,0:T(8,128)S(1)} collective-permute-done((f32[2,512,256]{2,1,0:T(8,128)S(1)}, f32[2,512,256]{2,1,0:T(8,128)S(1)}, u32[]{:S(2)}, u32[]{:S(2)}) %collective-permute-start.4) | collective-permute-done | bytes 1048608 | tf_op jit(solution)/shard_map/ppermute | solution.py:36
  129.3 1.2 fusion.5
  130.8 18.8 %all-reduce.6.cloned.1.call-done = f32[2,64,256]{2,1,0:T(8,128)} async-done(((f32[2,64,256]{2,1,0:T(8,128)}), f32[2,64,256]{2,1,0:T(8,128)}) %all-reduce.6.cloned.1.call-update) | async-done | bytes 131088 | tf_op jit(solution)/shard_map/psum | solution.py:139
  149.6 1.6 broadcast_select_fusion.4
  151.3 2.1 fusion.37
  153.3 71.8 %all-reduce.8.cloned.1.call-done = (f32[2,64,256]{2,1,0:T(8,128)}, f32[2,64,256]{2,1,0:T(8,128)}) async-done(((f32[2,64,256]{2,1,0:T(8,128)}, f32[2,64,256]{2,1,0:T(8,128)}), (f32[2,64,256]{2,1,0:T(8,128)}, f32[2,64,256]{2,1,0:T(8,128)})) %all-reduce.8.cloned.1.call-update) | async-done | bytes 262160 | tf_op jit(solution)/shard_map/psum | solution.py:41
  225.1 1.0 pad_maximum_fusion.6
  226.1 0.7 fusion.6
  227.1 2.7 %collective-permute-start.5 = (f32[2,64]{1,0:T(2,128)S(1)}, f32[2,64]{1,0:T(2,128)S(1)}, u32[]{:S(2)}, u32[]{:S(2)}) collective-permute-start(f32[2,64]{1,0:T(2,128)S(1)} %pad_maximum_fusion.7), channel_id=1, source_target_pairs={{2,0},{4,2},{6,4},{8,6},{10,8},{12,10},{14,12},{0,14},{3,1},{5,3},... | collective-permute-start | bytes 1544 | tf_op jit(solution)/shard_map/ppermute | solution.py:47
  229.8 0.7 dynamic-slice
  230.6 0.5 collective-permute-done.5
  231.4 0.7 fusion.61
  232.0 1.4 dynamic-update-slice
  233.5 22.8 %all-reduce.1 = (f32[1]{0:T(128)}, f32[8]{0:T(128)S(1)}) all-reduce(f32[1]{0:T(128)} %bitcast.19, f32[8]{0:T(128)S(1)} %dynamic-update-slice), channel_id=1, replica_groups=mesh['img'=2,'az'=8,'rg'=2] {'az'}, use_global_device_ids=true, to_apply=%region_10.11 | all-reduce | flops 9 | bytes 72 | tf_op jit(solution)/shard_map/psum | solution.py:168
  257.5 0.6 fusion.56
  (57 shorter events, 4.3 us)
Async XLA Ops:
  7.2 11.5 %copy-start.5 = (f32[2,512,256]{2,1,0:T(8,128)S(1)}, f32[2,512,256]{2,1,0:T(8,128)}, u32[]{:S(2)}) copy-start(f32[2,512,256]{2,1,0:T(8,128)} %param.8) | copy-start | bytes 3145732
  7.2 142.4 %all-reduce.6.cloned.1.call-start = ((), (), s32[]{:S(2)}) async-start(), calls=%async_computation | async-start | bytes 262144 | tf_op jit(solution)/shard_map/psum | solution.py:139
  8.4 10.3 %collective-permute-start = (f32[2,128,256]{2,1,0:T(8,128)S(1)}, f32[2,128,256]{2,1,0:T(8,128)S(1)}, u32[]{:S(2)}, u32[]{:S(2)}) collective-permute-start(f32[2,128,256]{2,1,0:T(8,128)S(1)} %get-tuple-element.53), channel_id=1, source_target_pairs={{0,1},{2,3},{4,5},{6,7},{8,9},{10,11},{12,13},{14,15},{16,17},{18,... | collective-permute-start | bytes 786440 | tf_op jit(solution)/shard_map/ppermute | solution.py:20
  10.7 7.9 %collective-permute-start.1 = (f32[2,128,256]{2,1,0:T(8,128)S(1)}, f32[2,128,256]{2,1,0:T(8,128)S(1)}, u32[]{:S(2)}, u32[]{:S(2)}) collective-permute-start(f32[2,128,256]{2,1,0:T(8,128)S(1)} %get-tuple-element.54), channel_id=1, source_target_pairs={{1,0},{3,2},{5,4},{7,6},{9,8},{11,10},{13,12},{15,14},{17,16},{19,... | collective-permute-start | bytes 786440 | tf_op jit(solution)/shard_map/ppermute | solution.py:22
  23.6 26.0 %collective-permute-start.2 = (f32[2,512,256]{2,1,0:T(8,128)S(1)}, f32[2,512,256]{2,1,0:T(8,128)S(1)}, u32[]{:S(2)}, u32[]{:S(2)}) collective-permute-start(f32[2,512,256]{2,1,0:T(8,128)S(1)} %pad_maximum_fusion.2), channel_id=1, source_target_pairs={{0,2},{2,0},{4,6},{6,4},{8,10},{10,8},{12,14},{14,12},{1,3},{3,1},... | collective-permute-start | bytes 3145736 | tf_op jit(solution)/shard_map/ppermute | solution.py:36
  49.8 27.4 %copy-start = (f32[1,512,256]{2,1,0:T(8,128)}, f32[1,512,256]{2,1,0:T(8,128)S(1)}, u32[]{:S(2)}) copy-start(f32[1,512,256]{2,1,0:T(8,128)S(1)} %get-tuple-element.51) | copy-start | bytes 1572868
  49.8 27.4 %copy-start.2 = (f32[1,512,256]{2,1,0:T(8,128)}, f32[1,512,256]{2,1,0:T(8,128)S(1)}, u32[]{:S(2)}) copy-start(f32[1,512,256]{2,1,0:T(8,128)S(1)} %get-tuple-element.52) | copy-start | bytes 1572868
  51.1 26.1 %collective-permute-start.3 = (f32[2,512,256]{2,1,0:T(8,128)}, f32[2,512,256]{2,1,0:T(8,128)}, u32[]{:S(2)}, u32[]{:S(2)}) collective-permute-start(f32[2,512,256]{2,1,0:T(8,128)} %subtract_select_fusion.2), channel_id=1, source_target_pairs={{0,4},{4,0},{2,6},{6,2},{8,12},{12,8},{10,14},{14,10},{1,5},{5,1},... | collective-permute-start | bytes 3145736 | tf_op jit(solution)/shard_map/ppermute | solution.py:36
  78.7 1.0 copy-start.1
  78.7 1.2 copy-start.3
  79.9 3.4 %copy-start.7 = (s32[64]{0:T(128)S(1)}, s32[64]{0:T(128)}, u32[]{:S(2)}) copy-start(s32[64]{0:T(128)} %param.13) | copy-start | bytes 772
  80.3 48.1 %collective-permute-start.4 = (f32[2,512,256]{2,1,0:T(8,128)S(1)}, f32[2,512,256]{2,1,0:T(8,128)S(1)}, u32[]{:S(2)}, u32[]{:S(2)}) collective-permute-start(f32[2,512,256]{2,1,0:T(8,128)S(1)} %subtract_select_fusion.1), channel_id=1, source_target_pairs={{0,8},{8,0},{2,10},{10,2},{4,12},{12,4},{6,14},{14,6},{1,9},{9,1},... | collective-permute-start | bytes 3145736 | tf_op jit(solution)/shard_map/ppermute | solution.py:36
  128.7 0.7 copy-start.6
  129.3 97.5 %copy-start.4 = (f32[2,512,256]{2,1,0:T(8,128)}, f32[2,512,256]{2,1,0:T(8,128)S(1)}, u32[]{:S(2)}) copy-start(f32[2,512,256]{2,1,0:T(8,128)S(1)} %subtract_select_fusion) | copy-start | bytes 3145732
  130.6 94.6 %all-reduce.8.cloned.1.call-start = ((), (), s32[]{:S(2)}) async-start(), calls=%async_computation.1 | async-start | bytes 524288 | tf_op jit(solution)/shard_map/psum | solution.py:41
  151.2 78.6 %copy-start.8 = (u32[32]{0:T(128)S(1)}, u32[32]{0:T(128)}, u32[]{:S(2)}) copy-start(u32[32]{0:T(128)} %constant.155) | copy-start | bytes 388
  227.1 4.0 %collective-permute-start.5 = (f32[2,64]{1,0:T(2,128)S(1)}, f32[2,64]{1,0:T(2,128)S(1)}, u32[]{:S(2)}, u32[]{:S(2)}) collective-permute-start(f32[2,64]{1,0:T(2,128)S(1)} %pad_maximum_fusion.7), channel_id=1, source_target_pairs={{2,0},{4,2},{6,4},{8,6},{10,8},{12,10},{14,12},{0,14},{3,1},{5,3},... | collective-permute-start | bytes 1544 | tf_op jit(solution)/shard_map/ppermute | solution.py:47
Sparse Core Ops, SparseCore 0:
  130.7 18.8 all-reduce.5
  153.1 71.9 all-reduce.7
where the time goes:
time: 268 us; the launch traced here: 265 us
  waiting for transfers between devices  183 us (68%)
  blocking collectives  22.8 us (9%)
  other arithmetic  16 us (6%)
  between operations  15.4 us (6%)
  starting transfers between devices  14.1 us (5%)
  local copies, waits for them, and re-layouts  7.39 us (3%)
  matrix products  5.92 us (2%)
    ppermute x3, waiting for transfers between devices, swapped(): return lax.ppermute(block, axis, route)  92.2 us
    psum x1, waiting for transfers between devices, broadcast(): return lax.psum(kept, axis)  71.8 us
    psum x1, blocking collectives, shards(): mean = lax.psum(local_total, 'az')[0] / total_cols  22.8 us
    psum x1, waiting for transfers between devices, shards(): gathered_rows = lax.psum(masked, 'rg')  18.8 us
    ppermute x3, starting transfers between devices, swapped(): return lax.ppermute(block, axis, route)  7.55 us
  transfers between devices with their start and end apart: 8, of which 6 were waited for; matrix products, arithmetic and copies ran while one was open for 4% of the time, Pallas kernels for 0%

commit v1 on v0

v1 whole, which is shorter than its diff:
```python
import functools
import math

import jax
import jax.numpy as jnp
import ml_dtypes
import numpy as np
from jax import lax
from jax.experimental import pallas as pl
from jax.experimental.pallas import tpu as pltpu
from jax.sharding import PartitionSpec as P

BLOCK = 128
SUB = 64
MESH = pl.DeviceIdType.MESH
BF = jnp.bfloat16
F32 = jnp.float32


def split_np(table):
    table = table.astype(np.float32)
    hi = table.astype(ml_dtypes.bfloat16)
    lo = (table - hi.astype(np.float32)).astype(ml_dtypes.bfloat16)
    return hi, lo


def make_tables(panels, cols):
    sections = panels.bit_length() - 1
    total = panels * cols
    k = np.arange(cols, dtype=np.int64)
    kk = np.where(k < cols // 2, k, k - cols)
    ang = 2.0 * math.pi * (np.outer(k, k) % cols) / cols
    c, s = np.cos(ang), np.sin(ang)
    dft = split_np(np.block([[c, -s], [s, c]]))
    ang = 2.0 * math.pi * (np.outer(kk, k) % total) / total
    c, s = np.cos(ang), np.sin(ang)
    inv = split_np(np.block([[c, s], [-s, c]]))
    count = 4 + 4 * sections
    factors = np.zeros((panels, -(-count // 8) * 8, cols))
    for d in range(panels):
        rev = int(format(d, "b").zfill(sections)[::-1], 2)
        ang = -2.0 * math.pi * (rev * k % total) / total
        factors[d, 0], factors[d, 1] = np.cos(ang), np.sin(ang)
        ang = np.where(k < cols // 2, 0.0, 2.0 * math.pi * rev / panels)
        factors[d, 2], factors[d, 3] = np.cos(ang), np.sin(ang)
        for bit in range(sections):
            half = 1 << bit
            turn = np.exp(-1j * math.pi * (d % half) / half)
            own, other = (1.0, turn) if not d >> bit & 1 else (-turn, 1.0)
            at = 4 + 4 * bit
            factors[d, at], factors[d, at + 1] = np.real(own), np.imag(own)
            factors[d, at + 2], factors[d, at + 3] = np.real(other), np.imag(other)
    ang = 2.0 * math.pi * (np.outer(np.arange(panels), kk) % panels) / panels
    phases = np.concatenate([np.cos(ang), np.sin(ang)], axis=1)
    ang = 2.0 * math.pi * (cols // 2 * k % total) / total
    edge = np.concatenate([np.cos(ang), np.sin(ang)])[None, :]
    return dft + inv + (factors.astype(np.float32), phases.astype(np.float32), edge.astype(np.float32))


def split(value):
    hi = value.astype(BF)
    return hi, (value - hi.astype(F32)).astype(BF)


def dot(a, b):
    return jnp.dot(a, b, preferred_element_type=F32)


def dot3(a, bhi, blo):
    hi, lo = split(a)
    return dot(hi, bhi) + (dot(hi, blo) + dot(lo, bhi))


def kernel(
    panels, rows, cols, scat,
    shift_ref, hist_ref, coef_ref, aux_ref, dhi_ref, dlo_ref, ihi_ref, ilo_ref, fac_ref, ph_ref, edge_ref,
    out_ref, phase_ref,
    halo, xhi, xlo, st, rv, auxt, pick, grx, g1, g1rx, g2, g2rx, acc, sig, nd, ndrx,
    halo_send, halo_recv, send, recv, gsend, grecv,
):
    sections = panels.bit_length() - 1
    nblocks = rows // BLOCK
    subs = BLOCK // SUB
    chunks = nblocks * subs
    total = panels * cols
    az = lax.axis_index("az")
    rg = lax.axis_index("rg")
    core = {"rg": 1 - rg}
    peers = []
    for bit in range(sections):
        half = 1 << bit
        low = 1 - az // half % 2
        peers.append({"az": az + half * (2 * low - 1)})
    barrier = pltpu.get_barrier_semaphore()
    for peer in [core] + peers:
        pl.semaphore_signal(barrier, inc=1, device_id=peer, device_id_type=MESH)
    pl.semaphore_wait(barrier, sections + 1)

    def block_row(p):
        return pl.multiple_of(BLOCK * (p + rg * (nblocks - 1 - 2 * p)), BLOCK)

    halo_copy = pltpu.make_async_remote_copy(
        src_ref=hist_ref.at[:, pl.ds(block_row(nblocks - 1), BLOCK), :], dst_ref=halo,
        send_sem=halo_send, recv_sem=halo_recv, device_id=core, device_id_type=MESH,
    )
    halo_copy.start()

    def chunk_rows(chunk):
        return pl.ds(pl.multiple_of(block_row(chunk // subs) + SUB * (chunk % subs), SUB), SUB)

    def piece(bit, chunk):
        part = chunk_rows(chunk)
        return pltpu.make_async_remote_copy(
            src_ref=st.at[bit, part, :], dst_ref=rv.at[bit, part, :],
            send_sem=send.at[bit, chunk], recv_sem=recv.at[bit, chunk],
            device_id=peers[bit], device_id_type=MESH,
        )

    pieces = [[piece(bit, chunk) for chunk in range(chunks)] for bit in range(sections)]

    def put(at, value):
        hi, lo = split(value)
        xhi[at, :] = hi
        xlo[at, :] = lo

    for b in range(nblocks + 1):
        auxt[b] = jnp.broadcast_to(aux_ref[b : b + 1, :], (BLOCK, BLOCK)).T
    outer = pl.ds(pl.multiple_of(rg * (rows + BLOCK), BLOCK), BLOCK)
    xhi[outer, :] = jnp.zeros((BLOCK, 2 * cols), BF)
    xlo[outer, :] = jnp.zeros((BLOCK, 2 * cols), BF)

    def load(p):
        base = block_row(p)
        at = pl.ds(base + BLOCK, BLOCK)
        here = pl.ds(base, BLOCK)
        put(at, jnp.concatenate([hist_ref[0, here, :], hist_ref[1, here, :]], axis=1))

    def spin(value, cosine, sine):
        re, im = value[:, :cols], value[:, cols:]
        return re * cosine - im * sine, re * sine + im * cosine

    def factor(row):
        return fac_ref[az, row : row + 1, :]

    lane3 = lax.broadcasted_iota(jnp.int32, (BLOCK, 3 * BLOCK), 1)
    row3 = lax.broadcasted_iota(jnp.int32, (BLOCK, 3 * BLOCK), 0)

    def first(p):
        base = block_row(p)
        b = p + rg * (nblocks - 1 - 2 * p)
        width = auxt[b]
        width = jnp.concatenate([width, width, width], axis=1)
        keep = jnp.abs(lane3 - BLOCK - row3 - shift_ref[b]) <= width
        weight = jnp.where(keep, coef_ref[pl.ds(base, BLOCK), :], 0.0)
        window = pl.ds(base, 3 * BLOCK)
        value = dot3(weight, xhi[window, :], xlo[window, :])
        value = dot3(value, dhi_ref[...], dlo_ref[...])
        re, im = spin(value, factor(0), factor(1))
        st[0, pl.ds(base, BLOCK), :cols] = re
        st[0, pl.ds(base, BLOCK), cols:] = im
        for sub in range(subs):
            pieces[0][subs * p + sub].start()

    def merged(bit, chunk):
        part = chunk_rows(chunk)
        pieces[bit][chunk].wait_recv()
        at = 4 + 4 * bit
        re, im = spin(st[bit, part, :], factor(at), factor(at + 1))
        re2, im2 = spin(rv[bit, part, :], factor(at + 2), factor(at + 3))
        return part, re + re2, im + im2

    def advance(bit, chunk):
        part, re, im = merged(bit, chunk)
        st[bit + 1, part, :cols] = re
        st[bit + 1, part, cols:] = im
        pieces[bit + 1][chunk].start()

    def finish(chunk):
        part, re, im = merged(sections - 1, chunk)
        out_ref[0, part, :] = re
        out_ref[1, part, :] = im

    half = scat // 2
    quarter = scat // 4
    wide = 2 * cols + BLOCK
    low0 = 1 - az % 2

    def link(src, dst, slot, peer):
        return pltpu.make_async_remote_copy(
            src_ref=src, dst_ref=dst, send_sem=gsend.at[slot], recv_sem=grecv.at[slot],
            device_id=peer, device_id_type=MESH,
        )

    def half_at(side):
        return pl.ds(pl.multiple_of(side * half, half), half)

    def quarter_at(side):
        return pl.ds(pl.multiple_of(side * quarter, quarter), quarter)

    links = [
        link(pick.at[half_at(1 - rg), :], grx, 0, core),
        link(g1.at[quarter_at(low0), :], g1rx, 1, peers[0]),
    ]
    for bit in range(1, sections):
        links.append(link(g2.at[bit - 1], g2rx.at[bit - 1], 1 + bit, peers[bit]))
    links.append(link(nd.at[0], ndrx.at[0], sections + 1, peers[0]))
    links.append(link(nd.at[1], ndrx.at[1], sections + 2, core))

    def g_pick():
        where = auxt[nblocks, 0:scat, :]
        where = jnp.concatenate([where] * (rows // BLOCK), axis=1)
        index = lax.broadcasted_iota(jnp.int32, (scat, rows), 1) + rg * rows
        onehot = (where == index).astype(F32).astype(BF)
        hi, lo = split(st[0])
        value = dot(onehot, hi) + dot(onehot, lo)
        re, im = spin(value, factor(2), factor(3))
        pick[:, :cols] = re
        pick[:, cols : 2 * cols] = im
        lane = lax.broadcasted_iota(jnp.int32, (scat, BLOCK), 1)
        mid = cols // 2
        re_mid = value[:, mid : mid + BLOCK]
        im_mid = value[:, cols + mid : cols + mid + BLOCK]
        pick[:, 2 * cols :] = jnp.where(lane == 0, re_mid, pltpu.roll(im_mid, 1, 1))
        links[0].start()

    def g_core():
        links[0].wait_recv()
        g1[...] = pick[half_at(rg), :] + grx[...]
        links[1].start()

    def g_bit0():
        links[1].wait_recv()
        g2[0] = g1[quarter_at(1 - low0), :] + g1rx[...]
        if sections > 1:
            links[2].start()

    def g_bit(bit):
        links[1 + bit].wait_recv()
        g2[bit] = g2[bit - 1] + g2rx[bit - 1]
        if bit < sections - 1:
            links[2 + bit].start()

    lane_q = lax.broadcasted_iota(jnp.int32, (quarter, cols), 1)

    def g_signal():
        value = g2[sections - 1]
        mine = pl.multiple_of(scat + rg * half + (1 - low0) * quarter, quarter)
        width = auxt[nblocks, pl.ds(mine, quarter), :]
        dist = jnp.where(lane_q < cols // 2, lane_q, cols - lane_q)
        inside = dist <= jnp.concatenate([width] * (cols // BLOCK), axis=1)
        re = jnp.where(inside, value[:, :cols], 0.0)
        im = jnp.where(inside, value[:, cols : 2 * cols], 0.0)
        ends = jnp.where(width >= cols // 2, value[:, 2 * cols :], 0.0)
        end_re, end_im = ends[:, 0:1], ends[:, 1:2]
        ec, es = edge_ref[:, :cols], edge_ref[:, cols:]
        extra = jnp.concatenate([end_re * ec - end_im * es, end_re * es + end_im * ec], axis=1)

        def fill(q, carry):
            c, s = ph_ref[pl.ds(q, 1), :cols], ph_ref[pl.ds(q, 1), cols:]
            at = pl.ds(pl.multiple_of(q * quarter, quarter), quarter)
            acc[at, :cols] = re * c - im * s
            acc[at, cols:] = re * s + im * c
            return carry

        lax.fori_loop(0, panels, fill, 0)
        sig[...] = dot3(acc[...], ihi_ref[...], ilo_ref[...])

        def reduce(q, carry):
            at = pl.ds(pl.multiple_of(q * quarter, quarter), quarter)
            nxt = pl.ds(pl.multiple_of((q + 1) % panels * quarter, quarter), quarter)
            now = sig[at, :] + extra
            after = sig[nxt, :] + extra
            now_re, now_im = now[:, :cols], now[:, cols:]
            last = lane_q == cols - 1
            next_re = jnp.where(last, pltpu.roll(after[:, :cols], cols - 1, 1), pltpu.roll(now_re, cols - 1, 1))
            next_im = jnp.where(last, pltpu.roll(after[:, cols:], cols - 1, 1), pltpu.roll(now_im, cols - 1, 1))
            numer = jnp.sum(now_re * next_im - now_im * next_re, axis=0, keepdims=True)
            denom = jnp.sum(now_re * now_re + now_im * now_im, axis=0, keepdims=True)
            nd[0, pl.ds(q, 1), :cols] = numer
            nd[0, pl.ds(q, 1), cols:] = denom
            return carry

        lax.fori_loop(0, panels, reduce, 0)
        links[sections + 1].start()

    def g_sum0():
        links[sections + 1].wait_recv()
        nd[1] = nd[0] + ndrx[0]
        links[sections + 2].start()

    def g_phase():
        links[sections + 2].wait_recv()
        sums = nd[1] + ndrx[1]
        grad = sums[:, :cols] / (sums[:, cols:] + 1e-06)
        before = lax.broadcasted_iota(jnp.int32, (cols, cols), 0) < lax.broadcasted_iota(jnp.int32, (cols, cols), 1)
        tri = before.astype(F32)
        within = jnp.dot(grad, tri, precision=lax.Precision.HIGHEST, preferred_element_type=F32)
        totals = jnp.sum(grad, axis=1, keepdims=True)
        panel = lax.broadcasted_iota(jnp.int32, (panels, 1), 0)
        ahead = jnp.sum(jnp.where(panel < az, totals, 0.0), axis=0, keepdims=True)
        mean = jnp.sum(totals, axis=0, keepdims=True) / total
        own = lax.broadcasted_iota(jnp.int32, (panels, cols), 0) == az
        run = jnp.sum(jnp.where(own, within, 0.0), axis=0, keepdims=True)
        n = (az * cols + lax.broadcasted_iota(jnp.int32, (1, cols), 1)).astype(F32)
        phase_ref[...] = ahead + run - n * mean

    tail = [g_pick, g_core, g_bit0]
    tail += [functools.partial(g_bit, bit) for bit in range(1, sections)]
    tail += [g_signal, g_sum0, g_phase]

    def halo_in():
        halo_copy.wait_recv()
        inner = pl.ds(pl.multiple_of((1 - rg) * (rows + BLOCK), BLOCK), BLOCK)
        put(inner, jnp.concatenate([halo[0], halo[1]], axis=1))

    load(0)
    load(1)
    first(0)
    load(2)
    first(1)
    for p in range(3, nblocks):
        load(p)
    done = 2
    for step in range(chunks + sections - 2):
        if step and step % 2 == 0 and done < nblocks:
            if done == nblocks - 1:
                halo_in()
            first(done)
            done += 1
        elif done == nblocks and tail:
            tail.pop(0)()
        for bit in range(sections - 1):
            chunk = step - bit
            if 0 <= chunk < chunks:
                advance(bit, chunk)
    for chunk in range(chunks):
        finish(chunk)
        if tail:
            tail.pop(0)()
    for step in tail:
        step()
    halo_copy.wait_send()
    for line in pieces:
        for copy in line:
            copy.wait_send()
    for copy in links:
        copy.wait_send()


def shards(history, coeffs, band_width, block_shift, scatter_rows, window_width):
    rows, cols = history.shape[1], history.shape[2]
    panels = lax.axis_size("az")
    sections = panels.bit_length() - 1
    scat = scatter_rows.shape[0]
    nblocks = rows // BLOCK
    chunks = rows // SUB
    small = jnp.concatenate([scatter_rows, window_width]).reshape(1, 2 * scat)
    aux = jnp.concatenate([band_width.reshape(nblocks, BLOCK), small], axis=0)
    tables = [jnp.asarray(t) for t in make_tables(panels, cols)]
    quarter = scat // 4
    wide = 2 * cols + BLOCK
    vmem = pl.BlockSpec(memory_space=pltpu.VMEM)
    state, phase = pl.pallas_call(
        functools.partial(kernel, panels, rows, cols, scat),
        out_shape=(
            jax.ShapeDtypeStruct((2, rows, cols), F32),
            jax.ShapeDtypeStruct((1, cols), F32),
        ),
        in_specs=[pl.BlockSpec(memory_space=pltpu.SMEM)] + [vmem] * 10,
        out_specs=(vmem, vmem),
        scratch_shapes=[
            pltpu.VMEM((2, BLOCK, cols), F32),
            pltpu.VMEM((rows + 2 * BLOCK, 2 * cols), BF),
            pltpu.VMEM((rows + 2 * BLOCK, 2 * cols), BF),
            pltpu.VMEM((sections, rows, 2 * cols), F32),
            pltpu.VMEM((sections, rows, 2 * cols), F32),
            pltpu.VMEM((nblocks + 1, BLOCK, BLOCK), jnp.int32),
            pltpu.VMEM((scat, wide), F32),
            pltpu.VMEM((scat // 2, wide), F32),
            pltpu.VMEM((scat // 2, wide), F32),
            pltpu.VMEM((quarter, wide), F32),
            pltpu.VMEM((sections, quarter, wide), F32),
            pltpu.VMEM((sections, quarter, wide), F32),
            pltpu.VMEM((panels * quarter, 2 * cols), F32),
            pltpu.VMEM((panels * quarter, 2 * cols), F32),
            pltpu.VMEM((2, panels, 2 * cols), F32),
            pltpu.VMEM((2, panels, 2 * cols), F32),
            pltpu.SemaphoreType.DMA,
            pltpu.SemaphoreType.DMA,
            pltpu.SemaphoreType.DMA((sections, chunks)),
            pltpu.SemaphoreType.DMA((sections, chunks)),
            pltpu.SemaphoreType.DMA((sections + 3,)),
            pltpu.SemaphoreType.DMA((sections + 3,)),
        ],
        compiler_params=pltpu.CompilerParams(
            collective_id=0, has_side_effects=True, vmem_limit_bytes=48 * 1024 * 1024
        ),
    )(block_shift, history, coeffs, aux, *tables)
    return state, phase.reshape(cols)


def solution(mesh):
    in_specs = (P(None, ("img", "rg"), "az"), P("rg", None), P("rg"), P("rg"), P("img"), P("img"))
    out_specs = (P(None, ("img", "rg"), "az"), P(("img", "az")))
    return jax.shard_map(shards, mesh=mesh, in_specs=in_specs, out_specs=out_specs, check_vma=False)
```

time: 268 us -> 80 us (0.30)
  waiting for transfers between devices: 183 us -> 0 us
  Pallas kernels: 0 us -> 68 us
  blocking collectives: 22.8 us -> 0 us
  between operations: 15.4 us -> 0.67 us
  other arithmetic: 16 us -> 1.47 us
  starting transfers between devices: 14.1 us -> 0 us
  matrix products: 5.92 us -> 0 us
    ppermute x6 -> x0, waiting for transfers between devices: 92.7 us -> none  [the longest x3 92.2 us: swapped(): return lax.ppermute(block, axis, route)]
    psum x2 -> x0, waiting for transfers between devices: 90.5 us -> none  [the longest x1 71.8 us: broadcast(): return lax.psum(kept, axis)]
    pallas_call x0 -> x1, Pallas kernels: none -> 68 us  [shards(): pl.pallas_call(functools.partial(kernel, panels, rows, cols, scat), out_s...]
    psum x1 -> x0, blocking collectives: 22.8 us -> none  [shards(): mean = lax.psum(local_total, 'az')[0] / total_cols]
    ppermute x6 -> x0, starting transfers between devices: 13.9 us -> none  [the longest x3 7.55 us: swapped(): return lax.ppermute(block, axis, route)]
    select_n x8 -> x0, other arithmetic: 6.77 us -> none  [the longest x3 1.91 us: shards(): state = jnp.where(lowbit, lower + moved, lower - moved)]
    dot_general x4 -> x0, matrix products: 5.92 us -> none  [the longest x1 2.2 us: shards(): jnp.einsum('bit,cbtn->cbin', weights, windows, precision=high)]
    unnamed x21 -> x22, local copies, waits for them, and re-layouts: 3.59 us -> 8.97 us
  transfers between devices with their start and end apart: 8 -> 0, of which waited for: 6 -> 0; matrix products, arithmetic and copies ran while one was open for 4% -> 0% of each run, Pallas kernels for 0% -> 0%
where the time goes in v1:
time: 80 us; the launch traced here: 79.1 us
  Pallas kernels  68 us (85%)
  local copies, waits for them, and re-layouts  8.97 us (11%)
  other arithmetic  1.47 us (2%)
    pallas_call x1, Pallas kernels, shards(): pl.pallas_call(functools.partial(kernel, panels, rows, cols, scat), out_s...  68 us
    unnamed x22, local copies, waits for them, and re-layouts  8.97 us

profile of v1, /device:TPU:0, one launch (start us, length us, event | category | flops | bytes accessed | tf_op | source)
XLA Modules:
  0.0 79.1 jit_solution(17495269205584787390)
XLA Ops:
  0.6 0.0 copy-start.7
  0.6 0.8 add_bitcast_fusion
  1.4 0.0 copy-start.8
  1.4 0.0 copy-start.9
  1.4 0.7 pad_add_fusion.aux_ref
  2.1 0.0 copy-done.7
  2.1 0.0 copy-done.8
  2.1 0.0 copy-done.9
  2.1 0.0 copy-start
  2.1 1.2 %copy-done = f32[2,512,256]{2,1,0:T(8,128)S(1)} copy-done((f32[2,512,256]{2,1,0:T(8,128)S(1)}, f32[2,512,256]{2,1,0:T(8,128)}, u32[]{:S(2)}) %copy-start) | copy-done | bytes 1048600
  3.4 0.0 copy-start.1
  3.4 1.1 %copy-done.1 = f32[512,384]{1,0:T(8,128)S(1)} copy-done((f32[512,384]{1,0:T(8,128)S(1)}, f32[512,384]{1,0:T(8,128)}, u32[]{:S(2)}) %copy-start.1) | copy-done | bytes 786456
  4.5 0.0 copy-start.2
  4.5 1.0 %copy-done.2 = bf16[512,512]{1,0:T(8,128)(2,1)S(1)} copy-done((bf16[512,512]{1,0:T(8,128)(2,1)S(1)}, bf16[512,512]{1,0:T(8,128)(2,1)}, u32[]{:S(2)}) %copy-start.2) | copy-done | bytes 524312
  5.5 0.0 copy-start.3
  5.5 1.0 %copy-done.3 = bf16[512,512]{1,0:T(8,128)(2,1)S(1)} copy-done((bf16[512,512]{1,0:T(8,128)(2,1)S(1)}, bf16[512,512]{1,0:T(8,128)(2,1)}, u32[]{:S(2)}) %copy-start.3) | copy-done | bytes 524312
  6.6 0.0 copy-start.4
  6.6 1.0 %copy-done.4 = bf16[512,512]{1,0:T(8,128)(2,1)S(1)} copy-done((bf16[512,512]{1,0:T(8,128)(2,1)S(1)}, bf16[512,512]{1,0:T(8,128)(2,1)}, u32[]{:S(2)}) %copy-start.4) | copy-done | bytes 524312
  7.6 0.0 copy-start.5
  7.6 1.0 %copy-done.5 = bf16[512,512]{1,0:T(8,128)(2,1)S(1)} copy-done((bf16[512,512]{1,0:T(8,128)(2,1)S(1)}, bf16[512,512]{1,0:T(8,128)(2,1)}, u32[]{:S(2)}) %copy-start.5) | copy-done | bytes 524312
  8.7 0.0 copy-start.6
  8.7 0.9 %copy-done.6 = f32[8,16,256]{2,1,0:T(8,128)S(1)} copy-done((f32[8,16,256]{2,1,0:T(8,128)S(1)}, f32[8,16,256]{2,1,0:T(8,128)}, u32[]{:S(2)}) %copy-start.6) | copy-done | bytes 131096
  9.6 68.0 %shard_map.140 = (f32[2,512,256]{2,1,0:T(8,128)S(1)}, f32[1,256]{1,0:T(1,128)S(1)}) custom-call(s32[4]{0:T(128)S(1)} %copy-done.9, f32[2,512,256]{2,1,0:T(8,128)S(1)} %copy-done, f32[512,384]{1,0:T(8,128)S(1)} %copy-done.1, s32[5,128]{1,0:T(8,128)S(1)} %pad_add_fusion.aux_ref, bf16[512,512]{1,0:T(8,128)(2,1)S(1)} %copy-done.5, ...), custom_call_target="tpu_custom_call" | custom-call | tf_op jit(solution)/shard_map/pallas_call | solution.py:363
  77.5 1.0 %copy.17 = f32[2,512,256]{2,1,0:T(8,128)} copy(f32[2,512,256]{2,1,0:T(8,128)S(1)} %get-tuple-element.8) | data formatting | bytes 2097152
  78.5 0.6 copy.18
Async XLA Ops:
  0.6 1.5 %copy-start.7 = (f32[8,512]{1,0:T(8,128)S(1)}, f32[8,512]{1,0:T(8,128)}, u32[]{:S(2)}) copy-start(f32[8,512]{1,0:T(8,128)} %constant.19.clone.ph_ref) | copy-start | bytes 49156
  1.4 0.7 copy-start.8
  1.4 0.7 copy-start.9
  2.1 1.2 %copy-start = (f32[2,512,256]{2,1,0:T(8,128)S(1)}, f32[2,512,256]{2,1,0:T(8,128)}, u32[]{:S(2)}) copy-start(f32[2,512,256]{2,1,0:T(8,128)} %hist_ref.1) | copy-start | bytes 3145732
  3.4 1.1 %copy-start.1 = (f32[512,384]{1,0:T(8,128)S(1)}, f32[512,384]{1,0:T(8,128)}, u32[]{:S(2)}) copy-start(f32[512,384]{1,0:T(8,128)} %coef_ref.1) | copy-start | bytes 2359300
  4.5 1.0 %copy-start.2 = (bf16[512,512]{1,0:T(8,128)(2,1)S(1)}, bf16[512,512]{1,0:T(8,128)(2,1)}, u32[]{:S(2)}) copy-start(bf16[512,512]{1,0:T(8,128)(2,1)} %constant.17.clone.ilo_ref) | copy-start | bytes 1572868
  5.5 1.0 %copy-start.3 = (bf16[512,512]{1,0:T(8,128)(2,1)S(1)}, bf16[512,512]{1,0:T(8,128)(2,1)}, u32[]{:S(2)}) copy-start(bf16[512,512]{1,0:T(8,128)(2,1)} %constant.16.clone.ihi_ref) | copy-start | bytes 1572868
  6.6 1.0 %copy-start.4 = (bf16[512,512]{1,0:T(8,128)(2,1)S(1)}, bf16[512,512]{1,0:T(8,128)(2,1)}, u32[]{:S(2)}) copy-start(bf16[512,512]{1,0:T(8,128)(2,1)} %constant.15.clone.dlo_ref) | copy-start | bytes 1572868
  7.6 1.0 %copy-start.5 = (bf16[512,512]{1,0:T(8,128)(2,1)S(1)}, bf16[512,512]{1,0:T(8,128)(2,1)}, u32[]{:S(2)}) copy-start(bf16[512,512]{1,0:T(8,128)(2,1)} %constant.14.clone.dhi_ref) | copy-start | bytes 1572868
  8.7 0.9 %copy-start.6 = (f32[8,16,256]{2,1,0:T(8,128)S(1)}, f32[8,16,256]{2,1,0:T(8,128)}, u32[]{:S(2)}) copy-start(f32[8,16,256]{2,1,0:T(8,128)} %constant.18.clone.fac_ref) | copy-start | bytes 393220

commit v2 on v1

--- a/solution.py
+++ b/solution.py
@@ -11,7 +11,7 @@
 from jax.sharding import PartitionSpec as P
 
 BLOCK = 128
-SUB = 64
+SUB = 32
 MESH = pl.DeviceIdType.MESH
 BF = jnp.bfloat16
 F32 = jnp.float32
@@ -73,8 +73,10 @@
 
 def kernel(
     panels, rows, cols, scat,
-    shift_ref, hist_ref, coef_ref, aux_ref, dhi_ref, dlo_ref, ihi_ref, ilo_ref, fac_ref, ph_ref, edge_ref,
+    shift_ref, hist_ref, coef_hbm, band_hbm, scat_hbm, wind_hbm, dhi_hbm, dlo_hbm, ihi_hbm, ilo_hbm,
+    fac_hbm, ph_hbm, edge_hbm,
     out_ref, phase_ref,
+    hist, coef_ref, band, scat_v, wind_v, dhi_ref, dlo_ref, ihi_ref, ilo_ref, fac_ref, ph_ref, edge_ref, local, done_rows, out_sem,
     halo, xhi, xlo, st, rv, auxt, pick, grx, g1, g1rx, g2, g2rx, acc, sig, nd, ndrx,
     halo_send, halo_recv, send, recv, gsend, grecv,
 ):
@@ -94,10 +96,34 @@
     barrier = pltpu.get_barrier_semaphore()
     for peer in [core] + peers:
         pl.semaphore_signal(barrier, inc=1, device_id=peer, device_id_type=MESH)
-    pl.semaphore_wait(barrier, sections + 1)
 
     def block_row(p):
         return pl.multiple_of(BLOCK * (p + rg * (nblocks - 1 - 2 * p)), BLOCK)
+
+    fetched = []
+
+    def fetch(src, dst):
+        copy = pltpu.make_async_copy(src, dst, local.at[len(fetched)])
+        copy.start()
+        fetched.append(copy)
+        return copy
+
+    hist_in, coef_in = [], []
+    band_in = fetch(band_hbm, band)
+    for p in range(nblocks):
+        at = pl.ds(block_row(p), BLOCK)
+        hist_in.append(fetch(hist_ref.at[:, at, :], hist.at[:, at, :]))
+        if p == 1:
+            coef_in.append(fetch(coef_hbm.at[pl.ds(block_row(0), BLOCK), :], coef_ref.at[pl.ds(block_row(0), BLOCK), :]))
+            dft_in = [fetch(dhi_hbm, dhi_ref), fetch(dlo_hbm, dlo_ref), fetch(fac_hbm.at[az], fac_ref)]
+    for p in range(1, nblocks):
+        at = pl.ds(block_row(p), BLOCK)
+        coef_in.append(fetch(coef_hbm.at[at, :], coef_ref.at[at, :]))
+    late_in = [
+        fetch(scat_hbm, scat_v), fetch(wind_hbm, wind_v), fetch(ihi_hbm, ihi_ref), fetch(ilo_hbm, ilo_ref),
+        fetch(ph_hbm, ph_ref), fetch(edge_hbm, edge_ref),
+    ]
+    pl.semaphore_wait(barrier, sections + 1)
 
     halo_copy = pltpu.make_async_remote_copy(
         src_ref=hist_ref.at[:, pl.ds(block_row(nblocks - 1), BLOCK), :], dst_ref=halo,
@@ -123,8 +149,9 @@
         xhi[at, :] = hi
         xlo[at, :] = lo
 
-    for b in range(nblocks + 1):
-        auxt[b] = jnp.broadcast_to(aux_ref[b : b + 1, :], (BLOCK, BLOCK)).T
+    band_in.wait()
+    for b in range(nblocks):
+        auxt[b] = jnp.broadcast_to(band[b : b + 1, :], (BLOCK, BLOCK)).T
     outer = pl.ds(pl.multiple_of(rg * (rows + BLOCK), BLOCK), BLOCK)
     xhi[outer, :] = jnp.zeros((BLOCK, 2 * cols), BF)
     xlo[outer, :] = jnp.zeros((BLOCK, 2 * cols), BF)
@@ -133,14 +160,15 @@
         base = block_row(p)
         at = pl.ds(base + BLOCK, BLOCK)
         here = pl.ds(base, BLOCK)
-        put(at, jnp.concatenate([hist_ref[0, here, :], hist_ref[1, here, :]], axis=1))
+        hist_in[p].wait()
+        put(at, jnp.concatenate([hist[0, here, :], hist[1, here, :]], axis=1))
 
     def spin(value, cosine, sine):
         re, im = value[:, :cols], value[:, cols:]
         return re * cosine - im * sine, re * sine + im * cosine
 
     def factor(row):
-        return fac_ref[az, row : row + 1, :]
+        return fac_ref[row : row + 1, :]
 
     lane3 = lax.broadcasted_iota(jnp.int32, (BLOCK, 3 * BLOCK), 1)
     row3 = lax.broadcasted_iota(jnp.int32, (BLOCK, 3 * BLOCK), 0)
@@ -148,6 +176,10 @@
     def first(p):
         base = block_row(p)
         b = p + rg * (nblocks - 1 - 2 * p)
+        coef_in[p].wait()
+        if p == 0:
+            for copy in dft_in:
+                copy.wait()
         width = auxt[b]
         width = jnp.concatenate([width, width, width], axis=1)
         keep = jnp.abs(lane3 - BLOCK - row3 - shift_ref[b]) <= width
@@ -175,10 +207,15 @@
         st[bit + 1, part, cols:] = im
         pieces[bit + 1][chunk].start()
 
+    stores = []
+
     def finish(chunk):
         part, re, im = merged(sections - 1, chunk)
-        out_ref[0, part, :] = re
-        out_ref[1, part, :] = im
+        done_rows[0, part, :] = re
+        done_rows[1, part, :] = im
+        copy = pltpu.make_async_copy(done_rows.at[:, part, :], out_ref.at[:, part, :], out_sem.at[chunk])
+        copy.start()
+        stores.append(copy)
 
     half = scat // 2
     quarter = scat // 4
@@ -207,6 +244,10 @@
     links.append(link(nd.at[1], ndrx.at[1], sections + 2, core))
 
     def g_pick():
+        for copy in late_in:
+            copy.wait()
+        small = jnp.concatenate([scat_v[...], wind_v[...]], axis=1)
+        auxt[nblocks] = jnp.broadcast_to(small, (BLOCK, BLOCK)).T
         where = auxt[nblocks, 0:scat, :]
         where = jnp.concatenate([where] * (rows // BLOCK), axis=1)
         index = lax.broadcasted_iota(jnp.int32, (scat, rows), 1) + rg * rows
@@ -322,7 +363,7 @@
         load(p)
     done = 2
     for step in range(chunks + sections - 2):
-        if step and step % 2 == 0 and done < nblocks:
+        if step and step % subs == 0 and done < nblocks:
             if done == nblocks - 1:
                 halo_in()
             first(done)
@@ -339,6 +380,8 @@
             tail.pop(0)()
     for step in tail:
         step()
+    for copy in stores:
+        copy.wait()
     halo_copy.wait_send()
     for line in pieces:
         for copy in line:
@@ -354,8 +397,6 @@
     scat = scatter_rows.shape[0]
     nblocks = rows // BLOCK
     chunks = rows // SUB
-    small = jnp.concatenate([scatter_rows, window_width]).reshape(1, 2 * scat)
-    aux = jnp.concatenate([band_width.reshape(nblocks, BLOCK), small], axis=0)
     tables = [jnp.asarray(t) for t in make_tables(panels, cols)]
     quarter = scat // 4
     wide = 2 * cols + BLOCK
@@ -366,9 +407,24 @@
             jax.ShapeDtypeStruct((2, rows, cols), F32),
             jax.ShapeDtypeStruct((1, cols), F32),
         ),
-        in_specs=[pl.BlockSpec(memory_space=pltpu.SMEM)] + [vmem] * 10,
-        out_specs=(vmem, vmem),
+        in_specs=[pl.BlockSpec(memory_space=pltpu.SMEM)] + [pl.BlockSpec(memory_space=pltpu.HBM)] * 12,
+        out_specs=(pl.BlockSpec(memory_space=pltpu.HBM), vmem),
         scratch_shapes=[
+            pltpu.VMEM((2, rows, cols), F32),
+            pltpu.VMEM((rows, 3 * BLOCK), F32),
+            pltpu.VMEM((nblocks, BLOCK), jnp.int32),
+            pltpu.VMEM((1, scat), jnp.int32),
+            pltpu.VMEM((1, scat), jnp.int32),
+            pltpu.VMEM((2 * cols, 2 * cols), BF),
+            pltpu.VMEM((2 * cols, 2 * cols), BF),
+            pltpu.VMEM((2 * cols, 2 * cols), BF),
+            pltpu.VMEM((2 * cols, 2 * cols), BF),
+            pltpu.VMEM(tables[4].shape[1:], F32),
+            pltpu.VMEM(tables[5].shape, F32),
+            pltpu.VMEM(tables[6].shape, F32),
+            pltpu.SemaphoreType.DMA((2 * nblocks + 10,)),
+            pltpu.VMEM((2, rows, cols), F32),
+            pltpu.SemaphoreType.DMA((chunks,)),
             pltpu.VMEM((2, BLOCK, cols), F32),
             pltpu.VMEM((rows + 2 * BLOCK, 2 * cols), BF),
             pltpu.VMEM((rows + 2 * BLOCK, 2 * cols), BF),
@@ -393,9 +449,12 @@
             pltpu.SemaphoreType.DMA((sections + 3,)),
         ],
         compiler_params=pltpu.CompilerParams(
-            collective_id=0, has_side_effects=True, vmem_limit_bytes=48 * 1024 * 1024
+            collective_id=0, has_side_effects=True, vmem_limit_bytes=56 * 1024 * 1024
         ),
-    )(block_shift, history, coeffs, aux, *tables)
+    )(
+        block_shift, history, coeffs, band_width.reshape(nblocks, BLOCK),
+        scatter_rows.reshape(1, scat), window_width.reshape(1, scat), *tables,
+    )
     return state, phase.reshape(cols)
 
 

time: 80 us -> 68.9 us (0.86)
  local copies, waits for them, and re-layouts: 8.97 us -> 2.83 us
  Pallas kernels: 68 us -> 65.3 us
  other arithmetic: 1.47 us -> 0 us
    unnamed x22 -> x4, local copies, waits for them, and re-layouts: 8.97 us -> 2.83 us
    pallas_call x1, Pallas kernels: 68 us -> 65.3 us  [shards(): pl.pallas_call(functools.partial(kernel, panels, rows, cols, scat), out_s...]
where the time goes in v2:
time: 68.9 us; the launch traced here: 68.8 us
  Pallas kernels  65.3 us (95%)
  local copies, waits for them, and re-layouts  2.83 us (4%)
    pallas_call x1, Pallas kernels, shards(): pl.pallas_call(functools.partial(kernel, panels, rows, cols, scat), out_s...  65.3 us
    unnamed x4, local copies, waits for them, and re-layouts  2.83 us

profile of v2, /device:TPU:0, one launch (start us, length us, event | category | flops | bytes accessed | tf_op | source)
XLA Modules:
  0.0 68.8 jit_solution(15405275765305997924)
XLA Ops:
  0.6 65.3 %shard_map.140 = (f32[2,512,256]{2,1,0:T(8,128)}, f32[1,256]{1,0:T(1,128)}) custom-call(s32[4]{0:T(128)} %shift_ref.1, f32[2,512,256]{2,1,0:T(8,128)} %hist_ref.1, f32[512,384]{1,0:T(8,128)} %coef_hbm.1, s32[4,128]{1,0:T(4,128)} %bitcast.4, s32[1,64]{1,0:T(1,128)} %bitcast.6, s32[1,64]{1,0:T(1,128)} %bitcast.7, bf16[512,512]{1,0:T(8,128)(2,1)} %constant.14.clone.dhi_hbm, ...), custom_call_target="tpu_custom_call" | custom-call | tf_op jit(solution)/shard_map/pallas_call | solution.py:404
  65.9 0.0 copy-start
  65.9 2.3 %copy.17 = f32[2,512,256]{2,1,0:T(8,128)} copy(f32[2,512,256]{2,1,0:T(8,128)} %get-tuple-element.8) | data formatting | bytes 2097152
  68.2 0.0 copy-done
  68.2 0.6 copy.18
Async XLA Ops:
  65.9 2.3 %copy-start = (f32[1,256]{1,0:T(1,128)S(1)}, f32[1,256]{1,0:T(1,128)}, u32[]{:S(2)}) copy-start(f32[1,256]{1,0:T(1,128)} %get-tuple-element.5) | copy-start | bytes 3076

commit v3 on v2

--- a/solution.py
+++ b/solution.py
@@ -12,6 +12,7 @@
 
 BLOCK = 128
 SUB = 32
+AHEAD = 3
 MESH = pl.DeviceIdType.MESH
 BF = jnp.bfloat16
 F32 = jnp.float32
@@ -76,7 +77,7 @@
     shift_ref, hist_ref, coef_hbm, band_hbm, scat_hbm, wind_hbm, dhi_hbm, dlo_hbm, ihi_hbm, ilo_hbm,
     fac_hbm, ph_hbm, edge_hbm,
     out_ref, phase_ref,
-    hist, coef_ref, band, scat_v, wind_v, dhi_ref, dlo_ref, ihi_ref, ilo_ref, fac_ref, ph_ref, edge_ref, local, done_rows, out_sem,
+    hist, coef_ref, band, scat_v, wind_v, dhi_ref, dlo_ref, ihi_ref, ilo_ref, fac_ref, ph_ref, edge_ref, local,
     halo, xhi, xlo, st, rv, auxt, pick, grx, g1, g1rx, g2, g2rx, acc, sig, nd, ndrx,
     halo_send, halo_recv, send, recv, gsend, grecv,
 ):
@@ -150,8 +151,6 @@
         xlo[at, :] = lo
 
     band_in.wait()
-    for b in range(nblocks):
-        auxt[b] = jnp.broadcast_to(band[b : b + 1, :], (BLOCK, BLOCK)).T
     outer = pl.ds(pl.multiple_of(rg * (rows + BLOCK), BLOCK), BLOCK)
     xhi[outer, :] = jnp.zeros((BLOCK, 2 * cols), BF)
     xlo[outer, :] = jnp.zeros((BLOCK, 2 * cols), BF)
@@ -180,7 +179,7 @@
         if p == 0:
             for copy in dft_in:
                 copy.wait()
-        width = auxt[b]
+        width = jnp.broadcast_to(band[pl.ds(b, 1), :], (BLOCK, BLOCK)).T
         width = jnp.concatenate([width, width, width], axis=1)
         keep = jnp.abs(lane3 - BLOCK - row3 - shift_ref[b]) <= width
         weight = jnp.where(keep, coef_ref[pl.ds(base, BLOCK), :], 0.0)
@@ -190,12 +189,22 @@
         re, im = spin(value, factor(0), factor(1))
         st[0, pl.ds(base, BLOCK), :cols] = re
         st[0, pl.ds(base, BLOCK), cols:] = im
-        for sub in range(subs):
-            pieces[0][subs * p + sub].start()
+        ready[0] = subs * (p + 1)
+        pump()
+
+    ready, limit, sent = [0], [AHEAD], [0]
+
+    def pump():
+        while sent[0] < min(ready[0], limit[0]):
+            pieces[0][sent[0]].start()
+            sent[0] += 1
 
     def merged(bit, chunk):
         part = chunk_rows(chunk)
         pieces[bit][chunk].wait_recv()
+        if bit == 0:
+            limit[0] = chunk + 1 + AHEAD
+            pump()
         at = 4 + 4 * bit
         re, im = spin(st[bit, part, :], factor(at), factor(at + 1))
         re2, im2 = spin(rv[bit, part, :], factor(at + 2), factor(at + 3))
@@ -207,15 +216,10 @@
         st[bit + 1, part, cols:] = im
         pieces[bit + 1][chunk].start()
 
-    stores = []
-
     def finish(chunk):
         part, re, im = merged(sections - 1, chunk)
-        done_rows[0, part, :] = re
-        done_rows[1, part, :] = im
-        copy = pltpu.make_async_copy(done_rows.at[:, part, :], out_ref.at[:, part, :], out_sem.at[chunk])
-        copy.start()
-        stores.append(copy)
+        out_ref[0, part, :] = re
+        out_ref[1, part, :] = im
 
     half = scat // 2
     quarter = scat // 4
@@ -357,18 +361,16 @@
     load(0)
     load(1)
     first(0)
-    load(2)
-    first(1)
-    for p in range(3, nblocks):
-        load(p)
-    done = 2
+    done = 1
     for step in range(chunks + sections - 2):
-        if step and step % subs == 0 and done < nblocks:
+        if step % 2 and done < nblocks:
             if done == nblocks - 1:
                 halo_in()
+            else:
+                load(done + 1)
             first(done)
             done += 1
-        elif done == nblocks and tail:
+        elif done == nblocks and tail and (step % 2 or len(tail) > sections + 3):
             tail.pop(0)()
         for bit in range(sections - 1):
             chunk = step - bit
@@ -380,8 +382,6 @@
             tail.pop(0)()
     for step in tail:
         step()
-    for copy in stores:
-        copy.wait()
     halo_copy.wait_send()
     for line in pieces:
         for copy in line:
@@ -404,11 +404,11 @@
     state, phase = pl.pallas_call(
         functools.partial(kernel, panels, rows, cols, scat),
         out_shape=(
-            jax.ShapeDtypeStruct((2, rows, cols), F32),
+            pltpu.VMEM((2, rows, cols), F32),
             jax.ShapeDtypeStruct((1, cols), F32),
         ),
         in_specs=[pl.BlockSpec(memory_space=pltpu.SMEM)] + [pl.BlockSpec(memory_space=pltpu.HBM)] * 12,
-        out_specs=(pl.BlockSpec(memory_space=pltpu.HBM), vmem),
+        out_specs=(vmem, vmem),
         scratch_shapes=[
             pltpu.VMEM((2, rows, cols), F32),
             pltpu.VMEM((rows, 3 * BLOCK), F32),
@@ -423,8 +423,6 @@
             pltpu.VMEM(tables[5].shape, F32),
             pltpu.VMEM(tables[6].shape, F32),
             pltpu.SemaphoreType.DMA((2 * nblocks + 10,)),
-            pltpu.VMEM((2, rows, cols), F32),
-            pltpu.SemaphoreType.DMA((chunks,)),
             pltpu.VMEM((2, BLOCK, cols), F32),
             pltpu.VMEM((rows + 2 * BLOCK, 2 * cols), BF),
             pltpu.VMEM((rows + 2 * BLOCK, 2 * cols), BF),

time: 68.9 us -> 66.1 us (0.959)
  Pallas kernels: 65.3 us -> 63.1 us
    pallas_call x1, Pallas kernels: 65.3 us -> 63.1 us  [shards(): pl.pallas_call(functools.partial(kernel, panels, rows, cols, scat), out_s...]
where the time goes in v3:
time: 66.1 us; the launch traced here: 66 us
  Pallas kernels  63.1 us (95%)
  local copies, waits for them, and re-layouts  2.19 us (3%)
    pallas_call x1, Pallas kernels, shards(): pl.pallas_call(functools.partial(kernel, panels, rows, cols, scat), out_s...  63.1 us
    unnamed x4, local copies, waits for them, and re-layouts  2.19 us

profile of v3, /device:TPU:0, one launch (start us, length us, event | category | flops | bytes accessed | tf_op | source)
XLA Modules:
  0.0 66.0 jit_solution(3204974271840562595)
XLA Ops:
  0.6 63.1 %shard_map.140 = (f32[2,512,256]{2,1,0:T(8,128)S(1)}, f32[1,256]{1,0:T(1,128)}) custom-call(s32[4]{0:T(128)} %shift_ref.1, f32[2,512,256]{2,1,0:T(8,128)} %hist_ref.1, f32[512,384]{1,0:T(8,128)} %coef_hbm.1, s32[4,128]{1,0:T(4,128)} %bitcast.4, s32[1,64]{1,0:T(1,128)} %bitcast.6, s32[1,64]{1,0:T(1,128)} %bitcast.7, bf16[512,512]{1,0:T(8,128)(2,1)} %constant.14.clone.dhi_hbm, ...), custom_call_target="tpu_custom_call" | custom-call | tf_op jit(solution)/shard_map/pallas_call | solution.py:404
  63.8 1.0 %copy.17 = f32[2,512,256]{2,1,0:T(8,128)} copy(f32[2,512,256]{2,1,0:T(8,128)S(1)} %get-tuple-element.6) | data formatting | bytes 2097152
  64.8 0.0 copy-start
  64.8 0.7 copy-done
  65.4 0.6 copy.18
Async XLA Ops:
  64.8 0.7 copy-start

commit v4 on v3

--- a/solution.py
+++ b/solution.py
@@ -184,13 +184,15 @@
         keep = jnp.abs(lane3 - BLOCK - row3 - shift_ref[b]) <= width
         weight = jnp.where(keep, coef_ref[pl.ds(base, BLOCK), :], 0.0)
         window = pl.ds(base, 3 * BLOCK)
-        value = dot3(weight, xhi[window, :], xlo[window, :])
-        value = dot3(value, dhi_ref[...], dlo_ref[...])
-        re, im = spin(value, factor(0), factor(1))
-        st[0, pl.ds(base, BLOCK), :cols] = re
-        st[0, pl.ds(base, BLOCK), cols:] = im
-        ready[0] = subs * (p + 1)
-        pump()
+        size = BLOCK // 2 if p == 0 else BLOCK
+        for top in range(0, BLOCK, size):
+            value = dot3(weight[top : top + size], xhi[window, :], xlo[window, :])
+            value = dot3(value, dhi_ref[...], dlo_ref[...])
+            re, im = spin(value, factor(0), factor(1))
+            st[0, pl.ds(base + top, size), :cols] = re
+            st[0, pl.ds(base + top, size), cols:] = im
+            ready[0] += size // SUB
+            pump()
 
     ready, limit, sent = [0], [AHEAD], [0]
 

time: 66.1 us -> 66 us (level)
  no operation moved by 1% of the time
where the time goes in v4:
time: 66 us; the launch traced here: 65.9 us
  Pallas kernels  63 us (95%)
  local copies, waits for them, and re-layouts  2.19 us (3%)
    pallas_call x1, Pallas kernels, shards(): pl.pallas_call(functools.partial(kernel, panels, rows, cols, scat), out_s...  63 us
    unnamed x4, local copies, waits for them, and re-layouts  2.19 us

profile of v4, /device:TPU:0, one launch (start us, length us, event | category | flops | bytes accessed | tf_op | source)
XLA Modules:
  0.0 65.9 jit_solution(14120874178565408282)
XLA Ops:
  0.6 63.0 %shard_map.140 = (f32[2,512,256]{2,1,0:T(8,128)S(1)}, f32[1,256]{1,0:T(1,128)}) custom-call(s32[4]{0:T(128)} %shift_ref.1, f32[2,512,256]{2,1,0:T(8,128)} %hist_ref.1, f32[512,384]{1,0:T(8,128)} %coef_hbm.1, s32[4,128]{1,0:T(4,128)} %bitcast.4, s32[1,64]{1,0:T(1,128)} %bitcast.6, s32[1,64]{1,0:T(1,128)} %bitcast.7, bf16[512,512]{1,0:T(8,128)(2,1)} %constant.14.clone.dhi_hbm, ...), custom_call_target="tpu_custom_call" | custom-call | tf_op jit(solution)/shard_map/pallas_call | solution.py:406
  63.7 1.0 %copy.17 = f32[2,512,256]{2,1,0:T(8,128)} copy(f32[2,512,256]{2,1,0:T(8,128)S(1)} %get-tuple-element.6) | data formatting | bytes 2097152
  64.7 0.0 copy-start
  64.7 0.7 copy-done
  65.3 0.6 copy.18
Async XLA Ops:
  64.7 0.7 copy-start
